TPU v7x, 32 devices: a whole 2x2x4 slice. The times are simulated.
32 devices in a mesh: gx: 8 (over y, x, core), gy: 4 (over z).
Axes of the slice: x: 2, y: 2, z: 4, core: 2. Of those that a mesh axis runs over, the one named last changes fastest.
Arguments:
- u_now: float32 [3, 6, 64, 512], P(None, None, 'gx', 'gy'), may hold values from -6 to 6
- u_prev: float32 [3, 6, 64, 512], P(None, None, 'gx', 'gy'), may hold values from -6 to 6
- lame_lambda: float32 [6, 64, 512], P(None, 'gx', 'gy'), may hold values from 0.5 to 1.5
- lame_mu: float32 [6, 64, 512], P(None, 'gx', 'gy'), may hold values from 0.3 to 1
- buoyancy: float32 [6, 64, 512], P(None, 'gx', 'gy'), may hold values from 0.5 to 1
- q_now: float32 [2048, 128], P(('gx', 'gy')), may hold values from -3 to 3
- q_prev: float32 [2048, 128], P(('gx', 'gy')), may hold values from -3 to 3
- archetype: int32 [2048], P(('gx', 'gy')), may hold values from 0 to 7
- stiffness: float32 [8, 128, 128], replicated, may hold values from -1.2 to 14, as said below
- couple: float32 [8, 3, 128], replicated, may hold values from -1.5 to 1.5
- counts: int32 [8, 4, 4], P('gx'), may hold values from 1 to 16, as said below
- footprint: int32 [8, 4, 256], P('gx', 'gy'), may hold values from 0 to 1023, as said below
Outputs:
- u_last: float32 [3, 6, 64, 512], P(None, None, 'gx', 'gy')
- u_before: float32 [3, 6, 64, 512], P(None, None, 'gx', 'gy')
- q_last: float32 [2048, 128], P(('gx', 'gy'))
- q_before: float32 [2048, 128], P(('gx', 'gy'))
Inputs may be any that keep to these rules, and one draw needn't show every extreme that they name: `stiffness`: symmetric, one matrix for each archetype. `counts`: at most 16; in every tile row some owner column receives 16 from every home column. `footprint`: the 4 cells of a slot form a 2 x 2 square of the home tile's surface, numbered x * 128 + y.
All inputs are finite; a program needn't handle non-finite values.
Results may differ from a plain program's by a relative error of at most 0.0001.
Values sent between devices are 32-bit elements; how exact they have to be, the bound alone decides.
A program may use at most 64 MiB of HBM per device.

v0:
```python
import functools

import jax
import jax.numpy as jnp
from jax import lax
from jax.experimental import pallas as pl
from jax.experimental.pallas import tpu as pltpu
from jax.sharding import PartitionSpec as P

FOOTPRINT_CELLS = 4
STEPS = 2
TIME_STEP = 0.25
RIM = 4
MESH = pl.DeviceIdType.MESH
F32 = jnp.float32
BF16 = jnp.bfloat16

X_DIRS = ((1, 0), (-1, 0))
Y_DIRS = ((-1, 1), (-1, -1), (0, 1), (0, -1), (1, 1), (1, -1))


def iota(shape, dim):
    return lax.broadcasted_iota(jnp.int32, shape, dim)


def split(value):
    high = value.astype(BF16)
    return high, (value - high.astype(F32)).astype(BF16)


def pack_x(fields):
    half = fields.shape[0] // 2
    first, second = fields[:half], fields[half:]
    upper = iota((1, 8, 128), 1) < RIM
    to_next = jnp.where(upper, pltpu.roll(first, RIM, 1), second)
    to_before = jnp.where(upper, first, pltpu.roll(second, RIM, 1))
    return to_next, to_before


def unpack_x(from_before, from_next):
    upper = iota((1, 8, 128), 1) < RIM
    first = jnp.where(upper, from_next, pltpu.roll(from_before, RIM, 1))
    second = jnp.where(upper, pltpu.roll(from_next, RIM, 1), from_before)
    return jnp.concatenate([first, second], axis=0)


def pack_y(fields):
    count = fields.shape[0]
    lane = iota((8, 128), 1)
    tiles = []
    for start in range(0, count, 16):
        tile = jnp.zeros((8, 128), F32)
        for k in range(start, min(start + 16, count)):
            place = 8 * (k - start)
            moved = pltpu.roll(fields[k], (place + RIM) % 128, 1)
            tile = jnp.where((lane >= place) & (lane < place + 8), moved, tile)
        tiles.append(tile)
    return jnp.stack(tiles)


def unpack_y(tiles, count):
    slabs = []
    for k in range(count):
        slabs.append(pltpu.roll(tiles[k // 16], (124 - 8 * (k % 16)) % 128, 1))
    return jnp.stack(slabs)


def slope(here, other, axis, both):
    size = here.shape[axis]
    place = iota((1,) * (here.ndim - 2) + (8, 128), axis)

    def shifted(mine, theirs, shift):
        entering = place < shift if shift > 0 else place >= size + shift
        return pltpu.roll(jnp.where(entering, theirs, mine), (-shift) % size, axis)

    def slope_of(mine, theirs):
        return 8.0 * (shifted(mine, theirs, 1) - shifted(mine, theirs, -1)) - (
            shifted(mine, theirs, 2) - shifted(mine, theirs, -2)
        )

    if both:
        return slope_of(here, other), slope_of(other, here)
    return slope_of(here, other)


def slope_z(field):
    nothing = jnp.zeros((2,) + field.shape[1:], F32)
    padded = jnp.concatenate([nothing, field, nothing], axis=0)
    n = field.shape[0]
    return 8.0 * (padded[3 : n + 3] - padded[1 : n + 1]) - (padded[4 : n + 4] - padded[:n])


def divergence(u, rim_x, rim_y, corner, lam, mu, lam_x, mu_x, lam_y, mu_y):
    ux, uy, uz = u[0], u[1], u[2]
    x_x, x_xh = slope(ux, rim_x[0], 1, True)
    y_x, y_xh = slope(uy, rim_x[1], 1, True)
    z_x, z_xh = slope(uz, rim_x[2], 1, True)
    x_y, x_yh = slope(ux, rim_y[0], 2, True)
    y_y, y_yh = slope(uy, rim_y[1], 2, True)
    z_y, z_yh = slope(uz, rim_y[2], 2, True)
    x_z, y_z, z_z = slope_z(ux), slope_z(uy), slope_z(uz)
    spread = lam * (x_x + y_y + z_z)
    s_xx = spread + 2.0 * mu * x_x
    s_yy = spread + 2.0 * mu * y_y
    s_zz = spread + 2.0 * mu * z_z
    s_xy = mu * (x_y + y_x)
    s_xz = mu * (x_z + z_x)
    s_yz = mu * (y_z + z_y)
    x_yr = slope(rim_x[0], corner[0], 2, False)
    y_yr = slope(rim_x[1], corner[1], 2, False)
    x_zr, z_zr = slope_z(rim_x[0]), slope_z(rim_x[2])
    s_xx_r = lam_x * (x_xh + y_yr + z_zr) + 2.0 * mu_x * x_xh
    s_xy_r = mu_x * (x_yr + y_xh)
    s_xz_r = mu_x * (x_zr + z_xh)
    x_xc = slope(rim_y[0], corner[0], 1, False)
    y_xc = slope(rim_y[1], corner[1], 1, False)
    y_zc, z_zc = slope_z(rim_y[1]), slope_z(rim_y[2])
    s_yy_c = lam_y * (x_xc + y_yh + z_zc) + 2.0 * mu_y * y_yh
    s_xy_c = mu_y * (x_yh + y_xc)
    s_yz_c = mu_y * (y_zc + z_yh)
    total_x = slope(s_xx, s_xx_r, 1, False) + slope(s_xy, s_xy_c, 2, False) + slope_z(s_xz)
    total_y = slope(s_xy, s_xy_r, 1, False) + slope(s_yy, s_yy_c, 2, False) + slope_z(s_yz)
    total_z = slope(s_xz, s_xz_r, 1, False) + slope(s_yz, s_yz_c, 2, False) + slope_z(s_zz)
    return jnp.stack([total_x, total_y, total_z])


def kernel(
    rows,
    owners,
    u_hbm,
    u_prev_hbm,
    lam_hbm,
    mu_hbm,
    buoy_hbm,
    q_hbm,
    q_prev_hbm,
    arch_hbm,
    stiff_hbm,
    couple_hbm,
    counts_hbm,
    cells_hbm,
    u_last_ref,
    u_before_ref,
    q_last_ref,
    q_before_ref,
    xs0,
    xs1,
    xr0,
    xr1,
    ys,
    yr,
    bs,
    br,
    table,
    u_ref,
    u_prev_ref,
    lam_ref,
    mu_ref,
    buoy_ref,
    q_ref,
    q_prev_ref,
    arch_ref,
    stiff_ref,
    couple_ref,
    counts_ref,
    cells_ref,
    loaded,
    x_send,
    x_recv,
    y_send,
    y_recv,
    b_send,
    b_recv,
):
    r, h = lax.axis_index("gx"), lax.axis_index("gy")
    nz = lam_ref.shape[0]
    slots = q_ref.shape[0]
    capacity = slots // owners
    kinds = stiff_ref.shape[0]
    freedoms = q_ref.shape[1]
    xs, xr = (xs0, xs1), (xr0, xr1)

    def target(direction):
        dx, dy = direction
        there = None
        for d, me, n in ((dx, r, rows), (dy, h, owners)):
            if d:
                ok = me + d < n if d > 0 else me > 0
                there = ok if there is None else there & ok
        return there, (r + dx, h + dy)

    def source(direction):
        return target((-direction[0], -direction[1]))

    peers = X_DIRS + tuple(d for d in Y_DIRS if d[0])

    for slot, direction in enumerate(X_DIRS):
        there, _ = source(direction)

        @pl.when(jnp.logical_not(there))
        def _(slot=slot):
            for buffer in xr:
                buffer[slot] = jnp.zeros(buffer.shape[1:], F32)

    for slot, direction in enumerate(Y_DIRS):
        there, _ = source(direction)

        @pl.when(jnp.logical_not(there))
        def _(slot=slot):
            for turn in range(STEPS):
                yr[turn, slot] = jnp.zeros(yr.shape[2:], F32)

    barrier = pltpu.get_barrier_semaphore()
    arrivals = jnp.int32(owners - 1)
    for direction in peers:
        there, device = target(direction)
        arrivals = arrivals + there.astype(jnp.int32)

        @pl.when(there)
        def _(device=device):
            pl.semaphore_signal(barrier, inc=1, device_id=device, device_id_type=MESH)

    for step in range(1, owners):
        other = lax.rem(h + step, owners)
        pl.semaphore_signal(barrier, inc=1, device_id=(r, other), device_id_type=MESH)

    loads = {}
    for source_ref, ref in (
        (u_hbm, u_ref),
        (lam_hbm, lam_ref),
        (mu_hbm, mu_ref),
        (cells_hbm, cells_ref),
        (counts_hbm, counts_ref),
        (q_hbm, q_ref),
        (arch_hbm, arch_ref),
        (couple_hbm, couple_ref),
        (stiff_hbm, stiff_ref),
        (q_prev_hbm, q_prev_ref),
        (u_prev_hbm, u_prev_ref),
        (buoy_hbm, buoy_ref),
    ):
        copy = pltpu.make_async_copy(source_ref, ref, loaded.at[len(loads)])
        copy.start()
        loads[id(ref)] = copy

    def load(ref):
        loads[id(ref)].wait()
        return ref[...]

    def x_copy(turn, slot, device):
        return pltpu.make_async_remote_copy(
            src_ref=xs[turn].at[slot],
            dst_ref=xr[turn].at[slot],
            send_sem=x_send.at[turn, slot],
            recv_sem=x_recv.at[turn, slot],
            device_id=device,
            device_id_type=MESH,
        )

    def y_copy(turn, slot, device):
        return pltpu.make_async_remote_copy(
            src_ref=ys.at[turn],
            dst_ref=yr.at[turn, slot],
            send_sem=y_send.at[turn, slot],
            recv_sem=y_recv.at[turn, slot],
            device_id=device,
            device_id_type=MESH,
        )

    def b_copy(turn, step):
        other = lax.rem(h + step, owners)
        return pltpu.make_async_remote_copy(
            src_ref=bs.at[turn, other],
            dst_ref=br.at[turn, h],
            send_sem=b_send.at[turn, step],
            recv_sem=b_recv.at[turn, step],
            device_id=(r, other),
            device_id_type=MESH,
        )

    def b_arrival(turn, step):
        other = lax.rem(h + owners - step, owners)
        return pltpu.make_async_remote_copy(
            src_ref=bs.at[turn, other],
            dst_ref=br.at[turn, other],
            send_sem=b_send.at[turn, step],
            recv_sem=b_recv.at[turn, step],
            device_id=(r, other),
            device_id_type=MESH,
        )

    def send_rims(turn):
        for copy, dirs in ((x_copy, X_DIRS), (y_copy, Y_DIRS)):
            for slot, direction in enumerate(dirs):
                there, device = target(direction)

                @pl.when(there)
                def _(copy=copy, slot=slot, device=device):
                    copy(turn, slot, device).start()

    def wait_rims(turn):
        for copy, dirs in ((x_copy, X_DIRS), (y_copy, Y_DIRS)):
            for slot, direction in enumerate(dirs):
                there, device = source(direction)

                @pl.when(there)
                def _(copy=copy, slot=slot, device=device):
                    copy(turn, slot, device).wait_recv()

    def wait_sends(turn):
        for copy, dirs in ((x_copy, X_DIRS), (y_copy, Y_DIRS)):
            for slot, direction in enumerate(dirs):
                there, device = target(direction)

                @pl.when(there)
                def _(copy=copy, slot=slot, device=device):
                    copy(turn, slot, device).wait_send()

        for step in range(1, owners):
            b_copy(turn, step).wait_send()

    def put_rims(turn, fields):
        to_next, to_before = pack_x(fields)
        xs[turn][0] = to_next
        xs[turn][1] = to_before
        tiles = pack_y(fields)
        ys[turn, : tiles.shape[0]] = tiles

    def take_rims(turn, count):
        rim_x = unpack_x(xr[turn][0], xr[turn][1])
        column = (iota((1, 8, 128), 2) & 7) < RIM
        before = jnp.where(column, yr[turn, 4], yr[turn, 5])
        beside = jnp.where(column, yr[turn, 2], yr[turn, 3])
        after = jnp.where(column, yr[turn, 0], yr[turn, 1])
        corner = jnp.where(iota((1, 8, 128), 1) < RIM, after, before)
        return rim_x, unpack_y(beside, count), unpack_y(corner, 3 * nz)

    u = load(u_ref)
    lam, mu = load(lam_ref) * (1.0 / 144.0), load(mu_ref) * (1.0 / 144.0)
    put_rims(0, jnp.concatenate([u.reshape(3 * nz, 8, 128), lam, mu], axis=0))
    pl.semaphore_wait(barrier, arrivals)
    send_rims(0)

    cells = load(cells_ref)[0].astype(F32)
    wide = (slots, slots * FOOTPRINT_CELLS)
    own = (iota(wide, 1) // FOOTPRINT_CELLS) == iota(wide, 0)
    corner_cell = jnp.min(jnp.where(own, cells, 1e9), axis=1, keepdims=True)
    corner_x = jnp.floor(corner_cell * (1.0 / 128.0))
    corner_y = corner_cell - 128.0 * corner_x
    lane = iota((slots, 128), 1)
    along_y = lane.astype(F32) - corner_y
    window_y = ((along_y == 0.0) | (along_y == 1.0)).astype(F32).astype(BF16)
    along_x = (lane & 7).astype(F32) - corner_x
    part = lane & 31
    slot_row = iota((slots, 1), 0)
    loads[id(counts_ref)].wait()
    row_counts = counts_ref[0, pl.ds(h, 1), :].astype(F32)
    pairs = (slots, owners)
    live_count = jnp.sum(
        jnp.where(iota(pairs, 0) // capacity == iota(pairs, 1), row_counts, 0.0),
        axis=1,
        keepdims=True,
    )
    live = (slot_row % capacity).astype(F32) < live_count
    weight = jnp.where(
        live & ((along_x == 0.0) | (along_x == 1.0)) & (part < 24), 1.0 / FOOTPRINT_CELLS, 0.0
    )
    square = (slots, slots)
    arch = jnp.sum(
        jnp.where(iota(square, 0) == iota(square, 1), load(arch_ref).astype(F32), 0.0),
        axis=1,
        keepdims=True,
    )
    is_kind = [arch == float(a) for a in range(kinds)]
    couple = load(couple_ref)
    coupling = []
    for c in range(3):
        chosen = jnp.zeros((slots, freedoms), F32)
        for a in range(kinds):
            chosen = jnp.where(is_kind[a], couple[c, a : a + 1, :], chosen)
        coupling.append(chosen)

    def surface_motion(field):
        surface = field[:, 0]
        high = surface.astype(BF16).astype(F32)
        nothing = jnp.zeros((8, 128), F32)
        stacked = jnp.concatenate(
            [high.reshape(24, 128), nothing, (surface - high).reshape(24, 128), nothing]
            + [nothing] * 8,
            axis=0,
        ).astype(BF16)
        gathered = lax.dot_general(
            window_y, stacked, (((1,), (1,)), ((), ())), preferred_element_type=F32
        )
        return gathered * weight

    def base_shear(state):
        shear = [jnp.sum(coupling[c] * state, axis=1, keepdims=True) for c in range(3)]
        return jnp.where(part < 8, shear[0], jnp.where(part < 16, shear[1], shear[2]))

    def send_buildings(turn, field, state):
        both = jnp.where(lane < 64, surface_motion(field), base_shear(state))
        both = both.reshape(owners, capacity, 128)
        bs[turn] = both
        br[turn, h] = bs[turn, h]
        for step in range(1, owners):
            b_copy(turn, step).start()

    def take_buildings(turn):
        for step in range(1, owners):
            b_arrival(turn, step).wait_recv()
        both = br[turn].reshape(slots, 128)
        drive = jnp.zeros((slots, freedoms), F32)
        for c in range(3):
            mine = (lane < 64) & (part >= 8 * c) & (part < 8 * c + 8)
            base = jnp.sum(jnp.where(mine, both, 0.0), axis=1, keepdims=True)
            drive = drive + coupling[c] * base
        pull = both * weight
        high = pull.astype(BF16).astype(F32)
        pull = jnp.where((lane & 32) == 0, high, pull - high)
        spread = lax.dot_general(
            pull.T.astype(BF16), window_y, (((1,), (0,)), ((), ())), preferred_element_type=F32
        )
        force = (spread[64:88] + spread[96:120]).reshape(3, 8, 128)
        return drive, force

    def stiff_term(state):
        high, low = split(state)
        stacked = jnp.concatenate([high.astype(F32), low.astype(F32)], axis=0)
        twice = jnp.concatenate([arch, arch], axis=0)
        spread = jnp.concatenate(
            [jnp.where(twice == float(a), stacked, 0.0).astype(BF16) for a in range(kinds)],
            axis=1,
        )
        product = jnp.dot(spread, table[...], preferred_element_type=F32)
        product = product[:, :freedoms] + product[:, freedoms:]
        return product[:slots] + product[slots:]

    q = load(q_ref)
    send_buildings(0, u, q)
    stiff_high, stiff_low = split(load(stiff_ref).reshape(kinds * freedoms, freedoms))
    table[:, :freedoms] = stiff_high
    table[:, freedoms:] = stiff_low
    stiff = stiff_term(q)
    u_old, q_old = load(u_prev_ref), load(q_prev_ref)
    gain = load(buoy_ref) * (TIME_STEP * TIME_STEP)
    count = 5 * nz
    lam_mu_x = lam_mu_y = None
    for turn in range(STEPS):
        drive, force = take_buildings(turn)
        q, q_old = 2.0 * q - q_old + (TIME_STEP * TIME_STEP) * (drive - stiff), q
        wait_rims(turn)
        rim_x, rim_y, corner = take_rims(turn, count)
        if turn == 0:
            lam_mu_x, lam_mu_y = rim_x[3 * nz :], rim_y[3 * nz :]
        shape = (3, nz, 8, 128)
        total = divergence(
            u,
            rim_x[: 3 * nz].reshape(shape),
            rim_y[: 3 * nz].reshape(shape),
            corner.reshape(shape),
            lam,
            mu,
            lam_mu_x[:nz],
            lam_mu_x[nz:],
            lam_mu_y[:nz],
            lam_mu_y[nz:],
        )
        total = jnp.concatenate([total[:, :1] + force[:, None], total[:, 1:]], axis=1)
        u, u_old = 2.0 * u - u_old + gain * total, u
        count = 3 * nz
        if turn + 1 < STEPS:
            put_rims(turn + 1, u.reshape(3 * nz, 8, 128))
            send_rims(turn + 1)
            send_buildings(turn + 1, u, q)
            u_before_ref[...] = u
            q_before_ref[...] = q
            stiff = stiff_term(q)
    u_last_ref[...] = u
    q_last_ref[...] = q
    for turn in range(STEPS):
        wait_sends(turn)


def shards(
    rows,
    owners,
    u_now,
    u_prev,
    lame_lambda,
    lame_mu,
    buoyancy,
    q_now,
    q_prev,
    archetype,
    stiffness,
    couple,
    counts,
    footprint,
):
    nz = lame_mu.shape[0]
    slots, freedoms = q_now.shape
    capacity = slots // owners
    kinds = stiffness.shape[0]
    pairs = (5 * nz) // 2, (3 * nz) // 2
    vmem = pl.BlockSpec(memory_space=pltpu.VMEM)
    hbm = pl.BlockSpec(memory_space=pltpu.HBM)
    dma = pltpu.SemaphoreType.DMA
    operands = (
        u_now,
        u_prev,
        lame_lambda,
        lame_mu,
        buoyancy,
        q_now,
        q_prev,
        archetype.reshape(1, slots),
        stiffness,
        couple.transpose(1, 0, 2),
        counts,
        footprint,
    )
    results = (
        jax.ShapeDtypeStruct(u_now.shape, F32),
        jax.ShapeDtypeStruct(u_now.shape, F32),
        jax.ShapeDtypeStruct(q_now.shape, F32),
        jax.ShapeDtypeStruct(q_now.shape, F32),
    )
    held = pl.pallas_call(
        functools.partial(kernel, rows, owners),
        out_shape=results,
        in_specs=[hbm] * len(operands),
        out_specs=(vmem,) * 4,
        scratch_shapes=[
            pltpu.VMEM((2, pairs[0], 8, 128), F32),
            pltpu.VMEM((2, pairs[1], 8, 128), F32),
            pltpu.VMEM((2, pairs[0], 8, 128), F32),
            pltpu.VMEM((2, pairs[1], 8, 128), F32),
            pltpu.VMEM((STEPS, 2, 8, 128), F32),
            pltpu.VMEM((STEPS, len(Y_DIRS), 2, 8, 128), F32),
            pltpu.VMEM((STEPS, owners, capacity, 128), F32),
            pltpu.VMEM((STEPS, owners, capacity, 128), F32),
            pltpu.VMEM((kinds * freedoms, 2 * freedoms), BF16),
        ]
        + [pltpu.VMEM(operand.shape, operand.dtype) for operand in operands]
        + [
            dma((len(operands),)),
            dma((STEPS, 2)),
            dma((STEPS, 2)),
            dma((STEPS, len(Y_DIRS))),
            dma((STEPS, len(Y_DIRS))),
            dma((STEPS, owners)),
            dma((STEPS, owners)),
        ],
        compiler_params=pltpu.CompilerParams(
            collective_id=0, has_side_effects=True, vmem_limit_bytes=60 * 1024 * 1024
        ),
    )(*operands)
    return pl.pallas_call(
        store,
        out_shape=results,
        in_specs=[vmem] * 4,
        out_specs=(hbm,) * 4,
        scratch_shapes=[dma((4,))],
    )(*held)


def store(*refs):
    copies = [
        pltpu.make_async_copy(refs[k], refs[4 + k], refs[8].at[k]) for k in range(4)
    ]
    for copy in copies:
        copy.start()
    for copy in copies:
        copy.wait()


def solution(mesh):
    return jax.shard_map(
        functools.partial(shards, mesh.shape["gx"], mesh.shape["gy"]),
        mesh=mesh,
        in_specs=(
            P(None, None, "gx", "gy"),
            P(None, None, "gx", "gy"),
            P(None, "gx", "gy"),
            P(None, "gx", "gy"),
            P(None, "gx", "gy"),
            P(("gx", "gy"), None),
            P(("gx", "gy"), None),
            P(("gx", "gy")),
            P(),
            P(),
            P("gx", None, None),
            P("gx", "gy", None),
        ),
        out_specs=(
            P(None, None, "gx", "gy"),
            P(None, None, "gx", "gy"),
            P(("gx", "gy"), None),
            P(("gx", "gy"), None),
        ),
        check_vma=False,
    )
```

profile of v0, /device:TPU:0, one launch (start us, length us, event | category | flops | bytes accessed | tf_op | source)
XLA Modules:
  0.0 18.1 jit_solution(13276195735842367244)
XLA Ops:
  0.6 15.8 %shard_map.147 = (f32[3,6,8,128]{3,2,1,0:T(8,128)}, f32[3,6,8,128]{3,2,1,0:T(8,128)}, f32[64,128]{1,0:T(8,128)}, f32[64,128]{1,0:T(8,128)}) custom-call(f32[3,6,8,128]{3,2,1,0:T(8,128)} %u_hbm.1, f32[3,6,8,128]{3,2,1,0:T(8,128)} %u_prev_hbm.1, f32[6,8,128]{2,1,0:T(8,128)} %lam_hbm.1, f32[6,8,128]{2,1,0:T(8,128)} %mu_hbm.1, f32[6,8,128]{2,1,0:T(8,128)} %buoy_hbm.1, ...), custom_call_target="tpu_custom_call" | custom-call | tf_op jit(solution)/shard_map/pallas_call | solution.py:529
  16.4 1.6 %shard_map.148 = (f32[3,6,8,128]{3,2,1,0:T(8,128)}, f32[3,6,8,128]{3,2,1,0:T(8,128)}, f32[64,128]{1,0:T(8,128)}, f32[64,128]{1,0:T(8,128)}) custom-call(f32[3,6,8,128]{3,2,1,0:T(8,128)} %get-tuple-element.8.refs_0_, f32[3,6,8,128]{3,2,1,0:T(8,128)} %get-tuple-element.9.refs_1_, f32[64,128]{1,0:T(8,128)} %get-tuple-element.10.refs_2_, ...), custom_call_target="tpu_custom_call" | custom-call | tf_op jit(solution)/shard_map/pallas_call | solution.py:559
where the time goes:
time: 18.3 us; the launch traced here: 18.1 us
  Pallas kernels  17.4 us (95%)
  between operations  0.64 us (3%)
    pallas_call x1, Pallas kernels, shards(): pl.pallas_call(functools.partial(kernel, rows, owners), out_shape=results...  15.8 us
    pallas_call x1, Pallas kernels, shards(): pl.pallas_call(store, out_shape=results, in_specs=[vmem] * 4, out_specs=(...  1.63 us

commit v1 on v0

--- a/solution.py
+++ b/solution.py
@@ -528,7 +528,7 @@
     )
     held = pl.pallas_call(
         functools.partial(kernel, rows, owners),
-        out_shape=results,
+        out_shape=tuple(pltpu.VMEM(result.shape, result.dtype) for result in results),
         in_specs=[hbm] * len(operands),
         out_specs=(vmem,) * 4,
         scratch_shapes=[
@@ -562,6 +562,7 @@
         in_specs=[vmem] * 4,
         out_specs=(hbm,) * 4,
         scratch_shapes=[dma((4,))],
+        compiler_params=pltpu.CompilerParams(vmem_limit_bytes=1024 * 1024),
     )(*held)
 
 

time: 18.3 us -> 16.6 us (0.907)
  Pallas kernels: 17.4 us -> 15.8 us
    pallas_call x1, Pallas kernels: 1.63 us -> 0.71 us  [shards(): pl.pallas_call(store, out_shape=results, in_specs=[vmem] * 4, out_specs=(...]
    pallas_call x1, Pallas kernels: 15.8 us -> 15.1 us  [shards(): pl.pallas_call(functools.partial(kernel, rows, owners), out_shape=tuple((...]
where the time goes in v1:
time: 16.6 us; the launch traced here: 16.5 us
  Pallas kernels  15.8 us (95%)
  between operations  0.64 us (4%)
    pallas_call x1, Pallas kernels, shards(): pl.pallas_call(functools.partial(kernel, rows, owners), out_shape=tuple((...  15.1 us
    pallas_call x1, Pallas kernels, shards(): pl.pallas_call(store, out_shape=results, in_specs=[vmem] * 4, out_specs=(...  0.71 us

profile of v1, /device:TPU:0, one launch (start us, length us, event | category | flops | bytes accessed | tf_op | source)
XLA Modules:
  0.0 16.5 jit_solution(4729029447353844150)
XLA Ops:
  0.6 15.1 %shard_map.147 = (f32[3,6,8,128]{3,2,1,0:T(8,128)S(1)}, f32[3,6,8,128]{3,2,1,0:T(8,128)S(1)}, f32[64,128]{1,0:T(8,128)S(1)}, f32[64,128]{1,0:T(8,128)S(1)}) custom-call(f32[3,6,8,128]{3,2,1,0:T(8,128)} %u_hbm.1, f32[3,6,8,128]{3,2,1,0:T(8,128)} %u_prev_hbm.1, f32[6,8,128]{2,1,0:T(8,128)} %lam_hbm.1, f32[6,8,128]{2,1,0:T(8,128)} %mu_hbm.1, ...), custom_call_target="tpu_custom_call" | custom-call | tf_op jit(solution)/shard_map/pallas_call | solution.py:529
  15.8 0.7 %shard_map.148 = (f32[3,6,8,128]{3,2,1,0:T(8,128)}, f32[3,6,8,128]{3,2,1,0:T(8,128)}, f32[64,128]{1,0:T(8,128)}, f32[64,128]{1,0:T(8,128)}) custom-call(f32[3,6,8,128]{3,2,1,0:T(8,128)S(1)} %get-tuple-element.8.refs_0_, f32[3,6,8,128]{3,2,1,0:T(8,128)S(1)} %get-tuple-element.9.refs_1_, f32[64,128]{1,0:T(8,128)S(1)} %get-tuple-element.10.refs_2_, ...), custom_call_target="tpu_custom_call" | custom-call | tf_op jit(solution)/shard_map/pallas_call | solution.py:559

commit v2 on v1

--- a/solution.py
+++ b/solution.py
@@ -226,14 +226,14 @@
 
     loads = {}
     for source_ref, ref in (
+        (cells_hbm, cells_ref),
+        (counts_hbm, counts_ref),
+        (arch_hbm, arch_ref),
+        (couple_hbm, couple_ref),
         (u_hbm, u_ref),
+        (q_hbm, q_ref),
         (lam_hbm, lam_ref),
         (mu_hbm, mu_ref),
-        (cells_hbm, cells_ref),
-        (counts_hbm, counts_ref),
-        (q_hbm, q_ref),
-        (arch_hbm, arch_ref),
-        (couple_hbm, couple_ref),
         (stiff_hbm, stiff_ref),
         (q_prev_hbm, q_prev_ref),
         (u_prev_hbm, u_prev_ref),
@@ -335,11 +335,6 @@
         corner = jnp.where(iota((1, 8, 128), 1) < RIM, after, before)
         return rim_x, unpack_y(beside, count), unpack_y(corner, 3 * nz)
 
-    u = load(u_ref)
-    lam, mu = load(lam_ref) * (1.0 / 144.0), load(mu_ref) * (1.0 / 144.0)
-    put_rims(0, jnp.concatenate([u.reshape(3 * nz, 8, 128), lam, mu], axis=0))
-    pl.semaphore_wait(barrier, arrivals)
-    send_rims(0)
 
     cells = load(cells_ref)[0].astype(F32)
     wide = (slots, slots * FOOTPRINT_CELLS)
@@ -398,13 +393,17 @@
         shear = [jnp.sum(coupling[c] * state, axis=1, keepdims=True) for c in range(3)]
         return jnp.where(part < 8, shear[0], jnp.where(part < 16, shear[1], shear[2]))
 
-    def send_buildings(turn, field, state):
+    def put_buildings(turn, field, state):
         both = jnp.where(lane < 64, surface_motion(field), base_shear(state))
         both = both.reshape(owners, capacity, 128)
         bs[turn] = both
         br[turn, h] = bs[turn, h]
-        for step in range(1, owners):
+
+    def send_buildings(turn):
+        for step in range(owners // 2, 0, -1):
             b_copy(turn, step).start()
+            if owners - step != step:
+                b_copy(turn, owners - step).start()
 
     def take_buildings(turn):
         for step in range(1, owners):
@@ -436,8 +435,13 @@
         product = product[:, :freedoms] + product[:, freedoms:]
         return product[:slots] + product[slots:]
 
-    q = load(q_ref)
-    send_buildings(0, u, q)
+    u, q = load(u_ref), load(q_ref)
+    put_buildings(0, u, q)
+    lam, mu = load(lam_ref) * (1.0 / 144.0), load(mu_ref) * (1.0 / 144.0)
+    put_rims(0, jnp.concatenate([u.reshape(3 * nz, 8, 128), lam, mu], axis=0))
+    pl.semaphore_wait(barrier, arrivals)
+    send_buildings(0)
+    send_rims(0)
     stiff_high, stiff_low = split(load(stiff_ref).reshape(kinds * freedoms, freedoms))
     table[:, :freedoms] = stiff_high
     table[:, freedoms:] = stiff_low
@@ -447,8 +451,6 @@
     count = 5 * nz
     lam_mu_x = lam_mu_y = None
     for turn in range(STEPS):
-        drive, force = take_buildings(turn)
-        q, q_old = 2.0 * q - q_old + (TIME_STEP * TIME_STEP) * (drive - stiff), q
         wait_rims(turn)
         rim_x, rim_y, corner = take_rims(turn, count)
         if turn == 0:
@@ -466,13 +468,16 @@
             lam_mu_y[:nz],
             lam_mu_y[nz:],
         )
+        drive, force = take_buildings(turn)
+        q, q_old = 2.0 * q - q_old + (TIME_STEP * TIME_STEP) * (drive - stiff), q
         total = jnp.concatenate([total[:, :1] + force[:, None], total[:, 1:]], axis=1)
         u, u_old = 2.0 * u - u_old + gain * total, u
         count = 3 * nz
         if turn + 1 < STEPS:
+            put_buildings(turn + 1, u, q)
+            send_buildings(turn + 1)
             put_rims(turn + 1, u.reshape(3 * nz, 8, 128))
             send_rims(turn + 1)
-            send_buildings(turn + 1, u, q)
             u_before_ref[...] = u
             q_before_ref[...] = q
             stiff = stiff_term(q)

time: 16.6 us -> 15.3 us (0.922)
  Pallas kernels: 15.8 us -> 14.5 us
    pallas_call x1, Pallas kernels: 15.1 us -> 13.8 us  [shards(): pl.pallas_call(functools.partial(kernel, rows, owners), out_shape=tuple((...]
where the time goes in v2:
time: 15.3 us; the launch traced here: 15.2 us
  Pallas kernels  14.5 us (95%)
  between operations  0.64 us (4%)
    pallas_call x1, Pallas kernels, shards(): pl.pallas_call(functools.partial(kernel, rows, owners), out_shape=tuple((...  13.8 us
    pallas_call x1, Pallas kernels, shards(): pl.pallas_call(store, out_shape=results, in_specs=[vmem] * 4, out_specs=(...  0.71 us

profile of v2, /device:TPU:0, one launch (start us, length us, event | category | flops | bytes accessed | tf_op | source)
XLA Modules:
  0.0 15.2 jit_solution(5495881931775638196)
XLA Ops:
  0.6 13.8 %shard_map.147 = (f32[3,6,8,128]{3,2,1,0:T(8,128)S(1)}, f32[3,6,8,128]{3,2,1,0:T(8,128)S(1)}, f32[64,128]{1,0:T(8,128)S(1)}, f32[64,128]{1,0:T(8,128)S(1)}) custom-call(f32[3,6,8,128]{3,2,1,0:T(8,128)} %u_hbm.1, f32[3,6,8,128]{3,2,1,0:T(8,128)} %u_prev_hbm.1, f32[6,8,128]{2,1,0:T(8,128)} %lam_hbm.1, f32[6,8,128]{2,1,0:T(8,128)} %mu_hbm.1, ...), custom_call_target="tpu_custom_call" | custom-call | tf_op jit(solution)/shard_map/pallas_call | solution.py:534
  14.5 0.7 %shard_map.148 = (f32[3,6,8,128]{3,2,1,0:T(8,128)}, f32[3,6,8,128]{3,2,1,0:T(8,128)}, f32[64,128]{1,0:T(8,128)}, f32[64,128]{1,0:T(8,128)}) custom-call(f32[3,6,8,128]{3,2,1,0:T(8,128)S(1)} %get-tuple-element.8.refs_0_, f32[3,6,8,128]{3,2,1,0:T(8,128)S(1)} %get-tuple-element.9.refs_1_, f32[64,128]{1,0:T(8,128)S(1)} %get-tuple-element.10.refs_2_, ...), custom_call_target="tpu_custom_call" | custom-call | tf_op jit(solution)/shard_map/pallas_call | solution.py:564

commit v3 on v2

--- a/solution.py
+++ b/solution.py
@@ -194,24 +194,12 @@
 
     peers = X_DIRS + tuple(d for d in Y_DIRS if d[0])
 
-    for slot, direction in enumerate(X_DIRS):
-        there, _ = source(direction)
-
-        @pl.when(jnp.logical_not(there))
-        def _(slot=slot):
-            for buffer in xr:
-                buffer[slot] = jnp.zeros(buffer.shape[1:], F32)
-
-    for slot, direction in enumerate(Y_DIRS):
-        there, _ = source(direction)
-
-        @pl.when(jnp.logical_not(there))
-        def _(slot=slot):
-            for turn in range(STEPS):
-                yr[turn, slot] = jnp.zeros(yr.shape[2:], F32)
-
     barrier = pltpu.get_barrier_semaphore()
     arrivals = jnp.int32(owners - 1)
+    for step in range(1, owners):
+        other = lax.rem(h + step, owners)
+        pl.semaphore_signal(barrier, inc=1, device_id=(r, other), device_id_type=MESH)
+
     for direction in peers:
         there, device = target(direction)
         arrivals = arrivals + there.astype(jnp.int32)
@@ -219,10 +207,6 @@
         @pl.when(there)
         def _(device=device):
             pl.semaphore_signal(barrier, inc=1, device_id=device, device_id_type=MESH)
-
-    for step in range(1, owners):
-        other = lax.rem(h + step, owners)
-        pl.semaphore_signal(barrier, inc=1, device_id=(r, other), device_id_type=MESH)
 
     loads = {}
     for source_ref, ref in (
@@ -242,6 +226,22 @@
         copy = pltpu.make_async_copy(source_ref, ref, loaded.at[len(loads)])
         copy.start()
         loads[id(ref)] = copy
+
+    for slot, direction in enumerate(X_DIRS):
+        there, _ = source(direction)
+
+        @pl.when(jnp.logical_not(there))
+        def _(slot=slot):
+            for buffer in xr:
+                buffer[slot] = jnp.zeros(buffer.shape[1:], F32)
+
+    for slot, direction in enumerate(Y_DIRS):
+        there, _ = source(direction)
+
+        @pl.when(jnp.logical_not(there))
+        def _(slot=slot):
+            for turn in range(STEPS):
+                yr[turn, slot] = jnp.zeros(yr.shape[2:], F32)
 
     def load(ref):
         loads[id(ref)].wait()

time: 15.3 us -> 15.3 us (level)
  no operation moved by 1% of the time
where the time goes in v3:
time: 15.3 us; the launch traced here: 15.1 us
  Pallas kernels  14.5 us (95%)
  between operations  0.64 us (4%)
    pallas_call x1, Pallas kernels, shards(): pl.pallas_call(functools.partial(kernel, rows, owners), out_shape=tuple((...  13.8 us
    pallas_call x1, Pallas kernels, shards(): pl.pallas_call(store, out_shape=results, in_specs=[vmem] * 4, out_specs=(...  0.71 us

profile of v3, /device:TPU:0, one launch (start us, length us, event | category | flops | bytes accessed | tf_op | source)
XLA Modules:
  0.0 15.1 jit_solution(1601525873746670202)
XLA Ops:
  0.6 13.8 %shard_map.147 = (f32[3,6,8,128]{3,2,1,0:T(8,128)S(1)}, f32[3,6,8,128]{3,2,1,0:T(8,128)S(1)}, f32[64,128]{1,0:T(8,128)S(1)}, f32[64,128]{1,0:T(8,128)S(1)}) custom-call(f32[3,6,8,128]{3,2,1,0:T(8,128)} %u_hbm.1, f32[3,6,8,128]{3,2,1,0:T(8,128)} %u_prev_hbm.1, f32[6,8,128]{2,1,0:T(8,128)} %lam_hbm.1, f32[6,8,128]{2,1,0:T(8,128)} %mu_hbm.1, ...), custom_call_target="tpu_custom_call" | custom-call | tf_op jit(solution)/shard_map/pallas_call | solution.py:534
  14.4 0.7 %shard_map.148 = (f32[3,6,8,128]{3,2,1,0:T(8,128)}, f32[3,6,8,128]{3,2,1,0:T(8,128)}, f32[64,128]{1,0:T(8,128)}, f32[64,128]{1,0:T(8,128)}) custom-call(f32[3,6,8,128]{3,2,1,0:T(8,128)S(1)} %get-tuple-element.8.refs_0_, f32[3,6,8,128]{3,2,1,0:T(8,128)S(1)} %get-tuple-element.9.refs_1_, f32[64,128]{1,0:T(8,128)S(1)} %get-tuple-element.10.refs_2_, ...), custom_call_target="tpu_custom_call" | custom-call | tf_op jit(solution)/shard_map/pallas_call | solution.py:564
